TPU v7x, 256 devices: a whole 4x4x8 slice. The times are simulated.
256 devices in a mesh: dp: 16 (over x, y), col: 16 (over z, core).
Axes of the slice: x: 4, y: 4, z: 8, core: 2. Of those that a mesh axis runs over, the one named last changes fastest.
Arguments:
- activations: bfloat16 [16, 1024, 4096], P('dp', 'col'), may hold values from -6 to 6
- out_grads: bfloat16 [16, 1024, 14336], P('dp', None, 'col'), may hold values from -0.0625 to 0.0625
- prev_factor: float32 [64, 14336], P(None, 'col'), may hold values from -0.046875 to 0.046875
Outputs:
- left_basis: float32 [64, 4096], replicated
- right_factor: float32 [64, 14336], P(None, 'col')
- residual: bfloat16 [16, 4096, 14336], P('dp', None, 'col')
All inputs are finite; a program needn't handle non-finite values.
Results may differ from a plain program's by a relative error of at most 0.00055.
Values may be sent and summed in bfloat16 or wider, within the bound.
A program may use at most 128 MiB of HBM per device.

v0:
```python
import jax
import jax.numpy as jnp
from jax import lax
from jax.sharding import PartitionSpec as P


def body(activations, out_grads, prev_factor):
    highest = lax.Precision.HIGHEST
    groups = lax.axis_size("dp")
    local_rows = activations[0]
    local_grads = out_grads[0]
    grad = lax.dot_general(
        lax.all_gather(local_rows, "col", axis=0, tiled=True),
        local_grads,
        (((0,), (0,)), ((), ())),
        preferred_element_type=jnp.float32,
    )
    partial_sketch = lax.dot_general(prev_factor, grad, (((1,), (1,)), ((), ())), precision=highest)
    sketch = lax.psum(partial_sketch, ("dp", "col")) / groups
    gram = jnp.dot(sketch, sketch.T, precision=highest)
    factor = jnp.linalg.cholesky(gram)
    left_basis = lax.linalg.triangular_solve(factor, sketch, left_side=True, lower=True)
    partial_factor = jnp.dot(left_basis, grad, precision=highest)
    right_factor = lax.psum(partial_factor, "dp") / groups
    approx = lax.dot_general(left_basis, right_factor, (((0,), (0,)), ((), ())), precision=highest)
    residual = (grad - approx).astype(jnp.bfloat16)
    return (left_basis, right_factor, residual[None])


def solution(mesh):
    placed = (P("dp", "col", None), P("dp", None, "col"), P(None, "col"))
    return jax.shard_map(
        body,
        mesh=mesh,
        in_specs=placed,
        out_specs=(P(), P(None, "col"), P("dp", None, "col")),
        check_vma=False,
    )
```

profile of v0, /device:TPU:1, one launch (start us, length us, event | category | flops | bytes accessed | tf_op | source)
XLA Modules:
  0.0 501.1 jit_solution(9011500730811085323)
XLA Ops:
  7.2 0.0 copy-start
  7.2 0.0 all-gather.3.cloned.1.call-start
  7.2 0.7 all-gather.3.cloned.1.call-update
  7.9 0.0 copy-start.4
  7.9 0.0 all-reduce.3.cloned.1.call-start
  8.0 62.0 %all-gather.3.cloned.1.call-done = bf16[1,1024,4096]{2,1,0:T(8,128)(2,1)} async-done(((bf16[1,64,4096]{2,1,0:T(8,128)(2,1)}), bf16[1,1024,4096]{2,1,0:T(8,128)(2,1)}) %all-gather.3.cloned.1.call-update) | async-done | bytes 8388624 | tf_op jit(solution)/shard_map/all_gather | solution.py:13
  70.0 0.0 copy-done
  70.0 11.7 %fusion = f32[4096,896]{1,0:T(8,128)S(1)} fusion(bf16[1,1024,4096]{2,1,0:T(8,128)(2,1)} %all-gather.3.cloned.1.call-done, bf16[1,1024,896]{2,1,0:T(8,128)(2,1)S(1)} %copy-done), kind=kOutput, calls=%fused_computation.1 | convolution fusion | flops 7516192768 | bytes 24903680 | tf_op jit(solution)/shard_map/dot_general | solution.py:12
  81.7 0.0 copy-start.1
  81.7 5.2 %copy-done.1 = f32[4096,896]{1,0:T(8,128)} copy-done((f32[4096,896]{1,0:T(8,128)}, f32[4096,896]{1,0:T(8,128)S(1)}, u32[]{:S(2)}) %copy-start.1) | copy-done | bytes 14680088
  86.9 0.0 copy-done.4
  86.9 15.5 %convolution_bitcast_fusion = f32[64,4096]{1,0:T(8,128)} fusion(f32[4096,896]{1,0:T(8,128)S(1)} %fusion, f32[64,896]{1,0:T(8,128)S(1)} %copy-done.4), kind=kOutput, calls=%fused_computation.4 | convolution fusion | flops 2818572288 | bytes 15958016 | tf_op jit(solution)/shard_map/dot_general | solution.py:18
  102.4 0.0 all-reduce.3.cloned.1.call-update
  102.4 0.3 all-reduce.5.cloned.1.call-start
  102.7 252.5 %all-reduce.3.cloned.1.call-done = f32[64,4096]{1,0:T(8,128)} async-done(((f32[64,4096]{1,0:T(8,128)}), f32[64,4096]{1,0:T(8,128)}) %all-reduce.3.cloned.1.call-update) | async-done | bytes 1048592 | tf_op jit(solution)/shard_map/psum | solution.py:19
  355.2 2.6 fusion.6
  357.8 0.1 copy.6
  357.9 5.8 %cholesky.16 = f32[64,64]{1,0:T(8,128)S(1)} custom-call(f32[64,64]{1,0:T(8,128)S(1)} %fusion.12), custom_call_target="Cholesky" | custom-call | tf_op jit(solution)/shard_map/jit(cholesky)/cholesky | solution.py:21
  363.8 0.6 compare_reduce_fusion
  364.4 0.7 fusion.10
  365.1 4.9 custom-call.6
  370.0 2.3 fusion.4
  372.2 0.0 copy-start.2
  372.2 12.7 %fusion.15 = f32[64,896]{1,0:T(8,128)} fusion(f32[64,4096]{1,0:T(8,128)S(1)} %fusion.4, f32[4096,896]{1,0:T(8,128)} %copy-done.1), kind=kOutput, calls=%fused_computation.24 | convolution fusion | flops 2818572288 | bytes 15958016 | tf_op jit(solution)/shard_map/dot_general | solution.py:23
  385.0 0.0 all-reduce.5.cloned.1.call-update
  385.0 92.8 %all-reduce.5.cloned.1.call-done = f32[64,896]{1,0:T(8,128)} async-done(((f32[64,896]{1,0:T(8,128)}), f32[64,896]{1,0:T(8,128)}) %all-reduce.5.cloned.1.call-update) | async-done | bytes 229392 | tf_op jit(solution)/shard_map/psum | solution.py:24
  477.8 1.0 broadcast_multiply_fusion
  478.7 0.0 copy-start.3
  478.8 15.8 %fusion.2 = bf16[1,4096,896]{2,1,0:T(8,128)(2,1)} fusion(f32[4096,896]{1,0:T(8,128)} %copy-done.1, f32[64,4096]{1,0:T(8,128)S(1)} %fusion.4, f32[64,896]{1,0:T(8,128)S(1)} %broadcast_multiply_fusion), kind=kOutput, calls=%fused_computation.3 | convolution fusion | flops 2825912320 | bytes 23298048 | tf_op jit(solution)/shard_map/dot_general | solution.py:25
  494.6 0.0 copy-done.2
  494.6 0.0 copy-done.3
  (2 shorter events, 0.0 us)
Async XLA Ops:
  7.2 62.8 %copy-start = (bf16[1,1024,896]{2,1,0:T(8,128)(2,1)S(1)}, bf16[1,1024,896]{2,1,0:T(8,128)(2,1)}, u32[]{:S(2)}) copy-start(bf16[1,1024,896]{2,1,0:T(8,128)(2,1)} %param.4) | copy-start | bytes 5505028
  7.2 62.8 %all-gather.3.cloned.1.call-start = ((), (), s32[]{:S(2)}) async-start(), calls=%async_computation.2 | async-start | bytes 8912896 | tf_op jit(solution)/shard_map/all_gather | solution.py:13
  7.9 79.0 %copy-start.4 = (f32[64,896]{1,0:T(8,128)S(1)}, f32[64,896]{1,0:T(8,128)}, u32[]{:S(2)}) copy-start(f32[64,896]{1,0:T(8,128)} %param.5) | copy-start | bytes 688132
  7.9 347.3 %all-reduce.3.cloned.1.call-start = ((), (), s32[]{:S(2)}) async-start(), calls=%async_computation | async-start | bytes 2097152 | tf_op jit(solution)/shard_map/psum | solution.py:19
  81.7 5.2 %copy-start.1 = (f32[4096,896]{1,0:T(8,128)}, f32[4096,896]{1,0:T(8,128)S(1)}, u32[]{:S(2)}) copy-start(f32[4096,896]{1,0:T(8,128)S(1)} %fusion) | copy-start | bytes 44040196
  102.4 375.4 %all-reduce.5.cloned.1.call-start = ((), (), s32[]{:S(2)}) async-start(), calls=%async_computation.1 | async-start | bytes 458752 | tf_op jit(solution)/shard_map/psum | solution.py:24
  372.2 122.3 %copy-start.2 = (f32[64,4096]{1,0:T(8,128)}, f32[64,4096]{1,0:T(8,128)S(1)}, u32[]{:S(2)}) copy-start(f32[64,4096]{1,0:T(8,128)S(1)} %fusion.4) | copy-start | bytes 3145732
  478.7 15.8 %copy-start.3 = (f32[64,896]{1,0:T(8,128)}, f32[64,896]{1,0:T(8,128)S(1)}, u32[]{:S(2)}) copy-start(f32[64,896]{1,0:T(8,128)S(1)} %broadcast_multiply_fusion) | copy-start | bytes 688132
Sparse Core Ops, SparseCore 0:
  9.8 60.1 all-gather.2
  102.5 252.6 all-reduce.2
  385.1 92.6 all-reduce.4
where the time goes:
time: 502 us; the launch traced here: 501 us
  waiting for transfers between devices  408 us (81%)
  matrix products  60.5 us (12%)
  between operations  13.8 us (3%)
  other arithmetic  13 us (3%)
  local copies, waits for them, and re-layouts  5.29 us (1%)
    psum x1, waiting for transfers between devices, body(): sketch = lax.psum(partial_sketch, ('dp', 'col')) / groups  253 us
    psum x1, waiting for transfers between devices, body(): right_factor = lax.psum(partial_factor, 'dp') / groups  92.8 us
    all_gather x1, waiting for transfers between devices, body(): lax.all_gather(local_rows, 'col', axis=0, tiled=True)  62 us
    dot_general x1, matrix products, body(): lax.dot_general(left_basis, right_factor, (((0,), (0,)), ((), ())), preci...  15.8 us
    dot_general x1, matrix products, body(): lax.dot_general(prev_factor, grad, (((1,), (1,)), ((), ())), precision=hi...  15.5 us
    dot_general x1, matrix products, body(): partial_factor = jnp.dot(left_basis, grad, precision=highest)  12.7 us
    dot_general x1, matrix products, body(): lax.dot_general(lax.all_gather(local_rows, 'col', axis=0, tiled=True), lo...  11.7 us
  transfers between devices with their start and end apart: 3, of which 3 were waited for; matrix products, arithmetic and copies ran while one was open for 0% of the time, Pallas kernels for 0%

commit v1 on v0

v1 whole, which is shorter than its diff:
```python
import functools

import jax
import jax.numpy as jnp
from jax import lax
from jax.experimental import pallas as pl
from jax.experimental.pallas import tpu as pltpu
from jax.sharding import PartitionSpec as P

MESH = pl.DeviceIdType.MESH
F32 = jnp.float32
BF16 = jnp.bfloat16
RANK = 64
HALF = 32
STAGES = ("rows", "proj", "zproj", "xysum", "zsum", "zgat", "xygat", "half", "zq", "xyfac", "xyfacg")


def split3(x):
    hi = x.astype(BF16)
    rest = x - hi.astype(F32)
    mid = rest.astype(BF16)
    lo = (rest - mid.astype(F32)).astype(BF16)
    return hi, mid, lo


def stack3(x):
    return jnp.concatenate(split3(x), axis=0)


def fold3(y, rows):
    return y[:rows] + (y[rows : 2 * rows] + y[2 * rows :])


NN = (((1,), (0,)), ((), ()))
NT = (((1,), (1,)), ((), ()))
TN = (((0,), (0,)), ((), ()))


def dot(a, b, dims):
    return lax.dot_general(a, b, dims, preferred_element_type=F32)


def inverse_factor(gram):
    n = gram.shape[0]
    row = lax.broadcasted_iota(jnp.int32, (n, n), 0)
    column = lax.broadcasted_iota(jnp.int32, (n, n), 1)
    eye = jnp.where(row == column, 1.0, 0.0).astype(F32)
    work = jnp.concatenate([eye, gram], axis=1)
    index = lax.broadcasted_iota(jnp.int32, (n, 1), 0)
    out = []
    for j in range(0, n, 2):
        r0, r1 = work[j : j + 1], work[j + 1 : j + 2]
        a = r0[:, n + j : n + j + 1]
        b = r0[:, n + j + 1 : n + j + 2]
        d = r1[:, n + j + 1 : n + j + 2]
        t = b / a
        s = d - b * t
        q1 = r1 - t * r0
        out.append(r0 * lax.rsqrt(a))
        out.append(q1 * lax.rsqrt(s))
        if j + 2 < n:
            c0 = work[:, n + j : n + j + 1]
            c1 = work[:, n + j + 1 : n + j + 2]
            below = index > j + 1
            m0 = jnp.where(below, c0 / a, 0.0)
            m1 = jnp.where(below, (c1 - c0 * t) / s, 0.0)
            work = work - m0 * r0 - m1 * q1
    return jnp.concatenate(out, axis=0)[:, :n]


def chain_kernel(
    groups, chips, a_ref, b_ref, p_ref, l_ref, r_ref,
    rows, halves, halves_in, psum, psum_in, part, part_in, tile, tile_in, tiles, full, qs, fac, fac_in, facs,
    *sems,
):
    send = dict(zip(STAGES, sems[: len(STAGES)]))
    recv = dict(zip(STAGES, sems[len(STAGES) : 2 * len(STAGES)]))
    local = sems[-1]
    g = lax.axis_index("dp")
    c = lax.axis_index("col")
    z, k = c // 2, c % 2
    wide = part.shape[2]
    sibling = (g, 2 * z + (1 - k))

    def z_peer(i):
        return lax.rem(z + i, chips)

    def g_peer(i):
        return lax.rem(g + i, groups)

    def copy(stage, slot, src, dst, device):
        return pltpu.make_async_remote_copy(
            src_ref=src, dst_ref=dst, send_sem=send[stage].at[slot], recv_sem=recv[stage].at[slot],
            device_id=device, device_id_type=MESH,
        )

    barrier = pltpu.get_barrier_semaphore()
    pl.semaphore_signal(barrier, inc=1, device_id=sibling, device_id_type=MESH)
    for i in range(1, chips):
        pl.semaphore_signal(barrier, inc=1, device_id=(g, 2 * z_peer(i) + k), device_id_type=MESH)
    for i in range(1, groups):
        pl.semaphore_signal(barrier, inc=1, device_id=(g_peer(i), c), device_id_type=MESH)

    own = pltpu.make_async_copy(a_ref, rows.at[pl.ds(64 * k, 64)], local.at[0])
    own.start()
    proj = fold3(dot(stack3(p_ref[...]), b_ref[...], NT), RANK)
    for kk in range(2):
        for zz in range(chips):
            halves[kk, zz] = proj[HALF * kk : HALF * (kk + 1), 128 * zz : 128 * (zz + 1)]
    pl.semaphore_wait(barrier, 1 + (chips - 1) + (groups - 1))

    send_half = copy("proj", 0, halves.at[1 - k], halves_in, sibling)
    send_half.start()
    send_rows = copy("rows", 0, a_ref, rows.at[pl.ds(64 * k, 64)], sibling)
    send_rows.start()
    send_half.wait_recv()

    psum[...] = halves[k] + halves_in[...]
    started = [send_half, send_rows]
    arriving = []
    for i in range(1, chips):
        to = z_peer(i)
        item = copy("zproj", i - 1, psum.at[to], psum_in.at[i - 1], (g, 2 * to + k))
        item.start()
        arriving.append(item)
    started += arriving
    mine = psum[z]
    for i, item in enumerate(arriving):
        item.wait_recv()
        mine = mine + psum_in[i]
    own.wait()
    send_rows.wait_recv()

    pieces = stack3(mine)
    arriving = []
    for i in range(1, groups + 1):
        to = lax.rem(g + i, groups)
        block = fold3(dot(pieces, rows[:, pl.ds(pl.multiple_of(wide * to, wide), wide)], NN), HALF)
        part[to] = block
        if i < groups:
            item = copy("xysum", i - 1, part.at[to], part_in.at[i - 1], (to, c))
            item.start()
            arriving.append(item)
    started += arriving
    mine = part[g]
    for i, item in enumerate(arriving):
        item.wait_recv()
        mine = mine + part_in[i]

    cols = wide // 128
    for j in range(chips):
        tile[j] = mine[8 * (j // cols) : 8 * (j // cols + 1), 128 * (j % cols) : 128 * (j % cols + 1)]
    arriving = []
    for i in range(1, chips):
        to = z_peer(i)
        item = copy("zsum", i - 1, tile.at[to], tile_in.at[i - 1], (g, 2 * to + k))
        item.start()
        arriving.append(item)
    started += arriving
    mine = tile[z]
    for i, item in enumerate(arriving):
        item.wait_recv()
        mine = mine + tile_in[i]
    tiles[z] = mine * (1.0 / groups)
    arriving = []
    for i in range(1, chips):
        item = copy("zgat", i - 1, tiles.at[z], tiles.at[z], (g, 2 * z_peer(i) + k))
        item.start()
        arriving.append(item)
    started += arriving
    for item in arriving:
        item.wait_recv()
    for j in range(chips):
        full[k, g, 8 * (j // cols) : 8 * (j // cols + 1), 128 * (j % cols) : 128 * (j % cols + 1)] = tiles[j]

    arriving = []
    for i in range(1, groups):
        item = copy("xygat", i - 1, full.at[k, g], full.at[k, g], (g_peer(i), c))
        item.start()
        arriving.append(item)
    started += arriving
    passed = [copy("half", 0, full.at[k, g], full.at[k, g], sibling)]
    passed[0].start()
    for i, item in enumerate(arriving):
        item.wait_recv()
        source = lax.rem(g + groups - (i + 1), groups)
        item = copy("half", i + 1, full.at[k, source], full.at[k, source], sibling)
        item.start()
        passed.append(item)
    started += passed
    for item in passed:
        item.wait_recv()

    gram = jnp.zeros((RANK, RANK), F32)
    for j in range(groups):
        block = jnp.concatenate([full[0, j], full[1, j]], axis=0)
        gram = gram + lax.dot_general(block, block, NT, precision=lax.Precision.HIGHEST, preferred_element_type=F32)
    inverse = inverse_factor(gram)
    q = jnp.zeros((3 * RANK, 128), F32)
    for j in range(groups):
        block = jnp.concatenate([full[0, j], full[1, j]], axis=0)
        block = lax.dot_general(inverse, block, NN, precision=lax.Precision.HIGHEST, preferred_element_type=F32)
        l_ref[:, wide * j : wide * (j + 1)] = block
        q = q + dot(stack3(block), rows[:, wide * j : wide * (j + 1)], NT)
    qs[z] = fold3(q, RANK)

    arriving = []
    for i in range(1, chips):
        item = copy("zq", i - 1, qs.at[z], qs.at[z], (g, 2 * z_peer(i) + k))
        item.start()
        arriving.append(item)
    started += arriving
    for item in arriving:
        item.wait_recv()
    q = jnp.concatenate([qs[j] for j in range(chips)], axis=1)
    factor = fold3(dot(stack3(q), b_ref[...], NN), RANK)

    tall = factor.shape[1] // 128
    for j in range(groups):
        if j < 2 * tall:
            fac[j] = factor[HALF * (j // tall) : HALF * (j // tall + 1), 128 * (j % tall) : 128 * (j % tall + 1)]
        else:
            fac[j] = jnp.zeros((HALF, 128), F32)
    arriving = []
    for i in range(1, groups):
        to = g_peer(i)
        item = copy("xyfac", i - 1, fac.at[to], fac_in.at[i - 1], (to, c))
        item.start()
        arriving.append(item)
    started += arriving
    mine = fac[g]
    for i, item in enumerate(arriving):
        item.wait_recv()
        mine = mine + fac_in[i]
    facs[g] = mine * (1.0 / groups)
    arriving = []
    for i in range(1, groups):
        item = copy("xyfacg", i - 1, facs.at[g], facs.at[g], (g_peer(i), c))
        item.start()
        arriving.append(item)
    started += arriving
    for item in arriving:
        item.wait_recv()
    for j in range(2 * tall):
        r_ref[HALF * (j // tall) : HALF * (j // tall + 1), 128 * (j % tall) : 128 * (j % tall + 1)] = facs[j]
    for item in started:
        item.wait_send()


def chain(groups, chips, rows, grads, prev):
    width, local = rows.shape[1], grads.shape[1]
    wide = width // groups
    counts = dict(
        rows=1, proj=1, zproj=chips - 1, xysum=groups - 1, zsum=chips - 1, zgat=chips - 1, xygat=groups - 1,
        half=groups, zq=chips - 1, xyfac=groups - 1, xyfacg=groups - 1,
    )
    dma = [pltpu.SemaphoreType.DMA((counts[s],)) for s in STAGES]
    vmem = pl.BlockSpec(memory_space=pltpu.VMEM)
    return pl.pallas_call(
        functools.partial(chain_kernel, groups, chips),
        out_shape=(jax.ShapeDtypeStruct((RANK, width), F32), jax.ShapeDtypeStruct((RANK, local), F32)),
        in_specs=[vmem] * 3,
        out_specs=(vmem, vmem),
        scratch_shapes=[
            pltpu.VMEM((128, width), BF16),
            pltpu.VMEM((2, chips, HALF, 128), F32),
            pltpu.VMEM((chips, HALF, 128), F32),
            pltpu.VMEM((chips, HALF, 128), F32),
            pltpu.VMEM((chips - 1, HALF, 128), F32),
            pltpu.VMEM((groups, HALF, wide), F32),
            pltpu.VMEM((groups - 1, HALF, wide), F32),
            pltpu.VMEM((chips, 8, 128), F32),
            pltpu.VMEM((chips - 1, 8, 128), F32),
            pltpu.VMEM((chips, 8, 128), F32),
            pltpu.VMEM((2, groups, HALF, wide), F32),
            pltpu.VMEM((chips, RANK, 128), F32),
            pltpu.VMEM((groups, HALF, 128), F32),
            pltpu.VMEM((groups - 1, HALF, 128), F32),
            pltpu.VMEM((groups, HALF, 128), F32),
            *dma,
            *dma,
            pltpu.SemaphoreType.DMA((1,)),
        ],
        compiler_params=pltpu.CompilerParams(collective_id=0, has_side_effects=True, vmem_limit_bytes=40 << 20),
        cost_estimate=pl.CostEstimate(flops=50_000_000_000, bytes_accessed=4 << 20, transcendentals=0),
        name="chain",
    )(rows, grads, prev)


def residual_kernel(a_ref, b_ref, l_ref, r_ref, out_ref, r3):
    @pl.when(pl.program_id(0) == 0)
    def _():
        hi, mid, _ = split3(r_ref[...])
        r3[0:RANK] = hi
        r3[RANK : 2 * RANK] = mid
        r3[2 * RANK :] = hi

    hi, mid, _ = split3(l_ref[...])
    left = jnp.concatenate([hi, hi, mid], axis=0)
    grad = dot(a_ref[...], b_ref[...], TN)
    out_ref[...] = (grad - dot(left, r3[...], TN)).astype(BF16)


def residual(gathered, grads, left, right, block=256):
    tokens, width = gathered.shape
    local = grads.shape[1]
    return pl.pallas_call(
        residual_kernel,
        grid=(width // block,),
        out_shape=jax.ShapeDtypeStruct((width, local), BF16),
        in_specs=[
            pl.BlockSpec((tokens, block), lambda i: (0, i)),
            pl.BlockSpec((tokens, local), lambda i: (0, 0)),
            pl.BlockSpec((RANK, block), lambda i: (0, i)),
            pl.BlockSpec((RANK, local), lambda i: (0, 0)),
        ],
        out_specs=pl.BlockSpec((block, local), lambda i: (i, 0)),
        scratch_shapes=[pltpu.VMEM((3 * RANK, local), BF16)],
        compiler_params=pltpu.CompilerParams(vmem_limit_bytes=58 << 20),
        name="residual",
    )(gathered, grads, left, right)


def body(groups, chips, activations, out_grads, prev_factor):
    rows, grads = activations[0], out_grads[0]
    gathered = lax.all_gather(rows, "col", axis=0, tiled=True)
    left, right = chain(groups, chips, rows, grads, prev_factor)
    return left, right, residual(gathered, grads, left, right)[None]


def solution(mesh):
    placed = (P("dp", "col", None), P("dp", None, "col"), P(None, "col"))
    return jax.shard_map(
        functools.partial(body, mesh.shape["dp"], mesh.shape["col"] // 2),
        mesh=mesh,
        in_specs=placed,
        out_specs=(P(), P(None, "col"), P("dp", None, "col")),
        check_vma=False,
    )
```

time: 502 us -> 123 us (0.25)
  waiting for transfers between devices: 408 us -> 0.68 us
  Pallas kernels: 0 us -> 101 us
  matrix products: 60.5 us -> 0 us
  other arithmetic: 13 us -> 0 us
    psum x2 -> x0, waiting for transfers between devices: 345 us -> none  [the longest x1 253 us: body(): sketch = lax.psum(partial_sketch, ('dp', 'col')) / groups]
    pallas_call x0 -> x2, Pallas kernels: none -> 101 us  [the longest x1 81.7 us: chain(): pl.pallas_call(functools.partial(chain_kernel, groups, chips), out_shape=...]
    all_gather x1, waiting for transfers between devices: 62 us -> 0.01 us  [body(): gathered = lax.all_gather(rows, 'col', axis=0, tiled=True)]
    dot_general x5 -> x0, matrix products: 58.3 us -> none  [the longest x1 15.8 us: body(): lax.dot_general(left_basis, right_factor, (((0,), (0,)), ((), ())), preci...]
    another operation x5 -> x0, other arithmetic: 12.1 us -> none  [the longest x3 6.52 us: body(): factor = jnp.linalg.cholesky(gram)]
  transfers between devices with their start and end apart: 3 -> 1, of which waited for: 3 -> 0; matrix products, arithmetic and copies ran while one was open for 0% -> 0% of each run, Pallas kernels for 0% -> 67%
where the time goes in v1:
time: 123 us
  Pallas kernels  101 us (82%)
  between operations  14.1 us (11%)
  local copies, waits for them, and re-layouts  6.79 us (6%)
    pallas_call x1, Pallas kernels, chain(): pl.pallas_call(functools.partial(chain_kernel, groups, chips), out_shape=...  81.7 us
    pallas_call x1, Pallas kernels, residual(): pl.pallas_call(residual_kernel, grid=(width // block,), out_shape=jax.Sha...  19.4 us
    unnamed x16, local copies, waits for them, and re-layouts  6.79 us
  transfers between devices with their start and end apart: 1, of which 0 were waited for; matrix products, arithmetic and copies ran while one was open for 0% of the time, Pallas kernels for 67%

profile of v1, /device:TPU:1, one launch (start us, length us, event | category | flops | bytes accessed | tf_op | source)
XLA Modules:
  0.0 122.7 jit_solution(8550678729822026223)
XLA Ops:
  7.2 0.0 all-gather.3.cloned.1.call-start
  7.2 0.7 all-gather.3.cloned.1.call-update
  7.9 0.0 copy-start.2
  7.9 1.5 %copy-done.2 = bf16[1,1024,896]{2,1,0:T(8,128)(2,1)S(1)} copy-done((bf16[1,1024,896]{2,1,0:T(8,128)(2,1)S(1)}, bf16[1,1024,896]{2,1,0:T(8,128)(2,1)}, u32[]{:S(2)}) %copy-start.2) | copy-done | bytes 1835032
  9.4 0.0 copy-start.5
  9.4 1.0 copy-done.5
  10.4 0.0 copy-start.6
  10.4 0.9 copy-done.6
  11.4 81.7 %chain.1 = (f32[64,4096]{1,0:T(8,128)S(1)}, f32[64,896]{1,0:T(8,128)S(1)}) custom-call(bf16[64,4096]{1,0:T(8,128)(2,1)S(1)} %bitcast.6, bf16[1024,896]{1,0:T(8,128)(2,1)S(1)} %bitcast.5, f32[64,896]{1,0:T(8,128)S(1)} %copy-done.6), custom_call_target="tpu_custom_call" | custom-call | flops 49999998976 | bytes 4194304 | tf_op jit(solution)/shard_map/chain/pallas_call | solution.py:259
  93.1 0.0 copy-start
  93.1 1.0 copy-done
  94.1 0.0 copy-start.3
  94.1 0.7 copy-done.3
  94.8 0.0 all-gather.3.cloned.1.call-done
  94.8 0.0 copy-start.1
  94.8 0.0 copy-start.4
  94.8 19.4 %residual.1 = bf16[4096,896]{1,0:T(8,128)(2,1)} custom-call(bf16[1024,4096]{1,0:T(8,128)(2,1)} %bitcast.7, bf16[1024,896]{1,0:T(8,128)(2,1)} %bitcast.4, f32[64,4096]{1,0:T(8,128)} %copy-done, f32[64,896]{1,0:T(8,128)} %copy-done.3), custom_call_target="tpu_custom_call" | custom-call | tf_op jit(solution)/shard_map/residual/pallas_call | solution.py:307
  114.2 0.0 copy-done.1
  114.2 1.0 copy.8
  115.2 0.0 copy-done.4
  115.2 0.7 copy.9
Async XLA Ops:
  7.2 87.6 %all-gather.3.cloned.1.call-start = ((), (), s32[]{:S(2)}) async-start(), calls=%async_computation | async-start | bytes 8912896 | tf_op jit(solution)/shard_map/all_gather | solution.py:326
  7.9 1.5 %copy-start.2 = (bf16[1,1024,896]{2,1,0:T(8,128)(2,1)S(1)}, bf16[1,1024,896]{2,1,0:T(8,128)(2,1)}, u32[]{:S(2)}) copy-start(bf16[1,1024,896]{2,1,0:T(8,128)(2,1)} %param.4) | copy-start | bytes 5505028
  9.4 1.0 copy-start.5
  10.4 0.9 copy-start.6
  93.1 1.0 copy-start
  94.1 0.7 copy-start.3
  94.8 19.4 %copy-start.1 = (f32[64,4096]{1,0:T(8,128)S(1)}, f32[64,4096]{1,0:T(8,128)}, u32[]{:S(2)}) copy-start(f32[64,4096]{1,0:T(8,128)} %copy-done) | copy-start | bytes 3145732
  94.8 20.4 %copy-start.4 = (f32[64,896]{1,0:T(8,128)S(1)}, f32[64,896]{1,0:T(8,128)}, u32[]{:S(2)}) copy-start(f32[64,896]{1,0:T(8,128)} %copy-done.3) | copy-start | bytes 688132
Sparse Core Ops, SparseCore 0:
  9.8 61.8 all-gather.2

commit v2 on v0

v2 whole, which is shorter than its diff:
```python
import functools

import jax
import jax.numpy as jnp
from jax import lax
from jax.experimental import pallas as pl
from jax.experimental.pallas import tpu as pltpu
from jax.sharding import PartitionSpec as P

MESH = pl.DeviceIdType.MESH
F32 = jnp.float32
BF16 = jnp.bfloat16
RANK = 64
HALF = 32
STAGES = ("proj", "zproj", "xysum", "zsum", "zgat", "xygat", "half", "zq", "qhalf", "xyfac", "xyfacg")
CHUNK = 16


def split3(x):
    hi = x.astype(BF16)
    rest = x - hi.astype(F32)
    mid = rest.astype(BF16)
    lo = (rest - mid.astype(F32)).astype(BF16)
    return hi, mid, lo


def stack3(x):
    return jnp.concatenate(split3(x), axis=0)


def fold3(y, rows):
    return y[:rows] + (y[rows : 2 * rows] + y[2 * rows :])


NN = (((1,), (0,)), ((), ()))
NT = (((1,), (1,)), ((), ()))
TN = (((0,), (0,)), ((), ()))


def dot(a, b, dims):
    return lax.dot_general(a, b, dims, preferred_element_type=F32)


def inverse_factor(gram):
    n = gram.shape[0]
    row = lax.broadcasted_iota(jnp.int32, (n, n), 0)
    column = lax.broadcasted_iota(jnp.int32, (n, n), 1)
    work = jnp.concatenate([jnp.where(row == column, 1.0, 0.0).astype(F32), gram], axis=1)
    out = []
    for top in range(0, n, 8):
        shape = (n - top, 2 * n)
        for p in range(0, 8, 2):
            j = n + top + p
            c0 = jnp.broadcast_to(work[:, j : j + 1], shape)
            c1 = jnp.broadcast_to(work[:, j + 1 : j + 2], shape)
            a, b, d = c0[p : p + 1], c0[p + 1 : p + 2], c1[p + 1 : p + 2]
            over_a = 1.0 / a
            t = b * over_a
            s = d - b * t
            r0 = work[p : p + 1]
            r1 = work[p + 1 : p + 2] - t * r0
            out.append(r0 * lax.rsqrt(a))
            out.append(r1 * lax.rsqrt(s))
            if j + 2 < 2 * n:
                work = work - c0 * (r0 * over_a) - (c1 - c0 * t) * (r1 * (1.0 / s))
        work = work[8:]
    return jnp.concatenate(out, axis=0)[:, :n]


def offsets(chips):
    order = [0]
    for step in range(1, chips // 2):
        order += [chips - step, step]
    return order + [chips // 2]


def main_kernel(
    groups, chips, a_ref, b_ref, p_ref, l_ref, r_ref, grad_ref,
    acts, grads, prev, halves, halves_in, psum, psum_in, part, part_in, tile, tile_in, tiles, full, qs, fac, fac_in, facs,
    *sems,
):
    count = len(STAGES)
    send = dict(zip(STAGES, sems[:count]))
    recv = dict(zip(STAGES, sems[count : 2 * count]))
    ring_send, ring_recv, side_send, side_recv, local = sems[2 * count :]
    g = lax.axis_index("dp")
    c = lax.axis_index("col")
    z, k = c // 2, c % 2
    wide = part.shape[2]
    width = acts.shape[1]
    cols = wide // 128
    sibling = (g, 2 * z + (1 - k))
    order = offsets(chips)
    slot_of = {offset: slot for slot, offset in enumerate(order)}

    def chip(offset):
        return lax.rem(z + offset, chips)

    def peer(offset):
        return (g, 2 * chip(offset) + k)

    def group(offset):
        return lax.rem(g + offset, groups)

    def copy(stage, slot, src, dst, device):
        return pltpu.make_async_remote_copy(
            src_ref=src, dst_ref=dst, send_sem=send[stage].at[slot], recv_sem=recv[stage].at[slot],
            device_id=device, device_id_type=MESH,
        )

    started = []

    def begin(item):
        item.start()
        started.append(item)
        return item

    chunks = 64 // CHUNK
    last = chips // 2

    def chunk(slot, core, q):
        return acts.at[pl.ds(pl.multiple_of(128 * slot + 64 * core + CHUNK * q, CHUNK), CHUNK)]

    def ring(way, hop, q):
        offset = hop if way else chips - hop
        source = slot_of[(offset - (1 if way else -1)) % chips]
        return pltpu.make_async_remote_copy(
            src_ref=chunk(source, k, q), dst_ref=chunk(slot_of[offset % chips], k, q),
            send_sem=ring_send.at[way, hop - 1, q], recv_sem=ring_recv.at[way, hop - 1, q],
            device_id=peer(chips - 1 if way else 1), device_id_type=MESH,
        )

    steps = []
    for hop in range(1, last):
        steps += [[(0, hop, q), (1, hop, q)] for q in range(chunks)]
    steps += [[(0, last, q), (1, last, q + chunks // 2)] for q in range(chunks // 2)]
    final = {item for step in steps for item in step if item[1] == last}
    served = [0]
    side = []

    def pass_on(slot, q, rows=CHUNK):
        ref = acts.at[pl.ds(pl.multiple_of(128 * slot + 64 * k + CHUNK * q, CHUNK), rows)]
        n = len(side)
        side.append(begin(pltpu.make_async_remote_copy(
            src_ref=ref, dst_ref=ref, send_sem=side_send.at[n], recv_sem=side_recv.at[n],
            device_id=sibling, device_id_type=MESH,
        )))

    ringing = {}

    def serve(upto):
        for step in steps[served[0] : upto]:
            for way, hop, q in step:
                ringing[way, hop, q].wait_recv()
                after = (way, hop + 1, q)
                if hop + 1 < last or after in final:
                    ringing[after] = begin(ring(*after))
            for way, hop, q in step:
                pass_on(slot_of[(hop if way else chips - hop) % chips], q)
        served[0] = max(served[0], upto)

    side_done = [0]

    def side_wait(upto):
        for item in side[side_done[0] : 1 + 2 * upto]:
            item.wait_recv()
        side_done[0] = max(side_done[0], 1 + 2 * upto)

    def multiply(low, high):
        rows = slice(128 * low, 128 * high)
        block = min(1024, width)

        @pl.loop(0, width // block)
        def _(m):
            at = pl.ds(pl.multiple_of(m * block, block), block)
            value = dot(acts[rows, at], grads[rows, :], TN)
            grad_ref[at, :] = value if low == 0 else grad_ref[at, :] + value

    barrier = pltpu.get_barrier_semaphore()
    pl.semaphore_signal(barrier, inc=1, device_id=sibling, device_id_type=MESH)
    for i in range(1, chips):
        pl.semaphore_signal(barrier, inc=1, device_id=peer(i), device_id_type=MESH)
    for i in range(1, groups):
        pl.semaphore_signal(barrier, inc=1, device_id=(group(i), c), device_id_type=MESH)

    loads = [pltpu.make_async_copy(p_ref, prev, local.at[0])]
    for s in range(chips):
        at = pl.ds(pl.multiple_of(128 * chip(order[s]), 128), 128)
        loads.append(pltpu.make_async_copy(b_ref.at[at], grads.at[pl.ds(128 * s, 128)], local.at[1 + s]))
    own = pltpu.make_async_copy(a_ref, acts.at[pl.ds(pl.multiple_of(64 * k, 64), 64)], local.at[1 + chips])
    for item in loads:
        item.start()
    own.start()
    for item in loads:
        item.wait()
    proj = fold3(dot(stack3(prev[...]), grads[...], NT), RANK)
    for kk in range(2):
        for s in range(chips):
            halves[kk, s] = proj[HALF * kk : HALF * (kk + 1), 128 * s : 128 * (s + 1)]
    own.wait()
    pl.semaphore_wait(barrier, 1 + (chips - 1) + (groups - 1))

    send_half = begin(copy("proj", 0, halves.at[1 - k], halves_in, sibling))
    pass_on(0, 0, 64)
    if EARLY:
        for q in range(chunks):
            for way in range(2):
                ringing[way, 1, q] = begin(ring(way, 1, q))
    send_half.wait_recv()

    psum[...] = halves[k] + halves_in[...]
    arriving = [
        begin(copy("zproj", i - 1, psum.at[slot_of[i]], psum_in.at[i - 1], peer(i))) for i in range(1, chips)
    ]
    if not EARLY:
        for q in range(chunks):
            for way in range(2):
                ringing[way, 1, q] = begin(ring(way, 1, q))
    mine = psum[0]
    for i, item in enumerate(arriving):
        item.wait_recv()
        mine = mine + psum_in[i]
    side_wait(0)

    pieces = stack3(mine)
    arriving = []
    for i in range(1, groups + 1):
        to = group(i)
        part[to] = fold3(dot(pieces, acts[:128, pl.ds(pl.multiple_of(wide * to, wide), wide)], NN), HALF)
        if i < groups:
            arriving.append(begin(copy("xysum", i - 1, part.at[to], part_in.at[i - 1], (to, c))))
    serve(PLAN[0])
    mine = part[g]
    for i, item in enumerate(arriving):
        item.wait_recv()
        mine = mine + part_in[i]

    for j in range(chips):
        tile[j] = mine[8 * (j // cols) : 8 * (j // cols + 1), 128 * (j % cols) : 128 * (j % cols + 1)]
    arriving = [begin(copy("zsum", i - 1, tile.at[chip(i)], tile_in.at[i - 1], peer(i))) for i in range(1, chips)]
    serve(PLAN[1])
    mine = tile[z]
    for i, item in enumerate(arriving):
        item.wait_recv()
        mine = mine + tile_in[i]
    tiles[z] = mine * (1.0 / groups)
    arriving = [begin(copy("zgat", i - 1, tiles.at[z], tiles.at[z], peer(i))) for i in range(1, chips)]
    serve(PLAN[2])
    for item in arriving:
        item.wait_recv()
    for j in range(chips):
        full[k, g, 8 * (j // cols) : 8 * (j // cols + 1), 128 * (j % cols) : 128 * (j % cols + 1)] = tiles[j]

    arriving = [begin(copy("xygat", i - 1, full.at[k, g], full.at[k, g], (group(i), c))) for i in range(1, groups)]
    passed = []

    def meet(q, source):
        at = pl.ds(pl.multiple_of(wide * source, wide), wide)
        return q + dot(stack3(full[k, source]), acts[:128, at], NT)

    passed.append(begin(copy("half", 0, full.at[k, g], full.at[k, g], sibling)))
    q = meet(jnp.zeros((3 * HALF, 128), F32), g)
    serve(PLAN[3])
    for i, item in enumerate(arriving):
        item.wait_recv()
        source = group(groups - (i + 1))
        passed.append(begin(copy("half", i + 1, full.at[k, source], full.at[k, source], sibling)))
        q = meet(q, source)
    qs[k, 0] = fold3(q, HALF)

    arriving = [
        begin(copy("zq", i - 1, qs.at[k, 0], qs.at[k, slot_of[chips - i]], peer(i))) for i in range(1, chips)
    ]
    crossing = [begin(copy("qhalf", 0, qs.at[k, 0], qs.at[k, 0], sibling))]
    serve(PLAN[4])
    side_wait(served[0])
    multiply(0, chips // 2)
    serve(PLAN[5])
    for i, item in enumerate(arriving):
        item.wait_recv()
        here = qs.at[k, slot_of[chips - (i + 1)]]
        crossing.append(begin(copy("qhalf", i + 1, here, here, sibling)))
    for item in crossing:
        item.wait_recv()
    q = jnp.concatenate([jnp.concatenate([qs[0, s], qs[1, s]], axis=0) for s in range(chips)], axis=1)
    factor = fold3(dot(stack3(q), grads[...], NN), RANK)

    tall = factor.shape[1] // 128
    for j in range(groups):
        if j < 2 * tall:
            fac[j] = factor[HALF * (j // tall) : HALF * (j // tall + 1), 128 * (j % tall) : 128 * (j % tall + 1)]
        else:
            fac[j] = jnp.zeros((HALF, 128), F32)
    arriving = [
        begin(copy("xyfac", i - 1, fac.at[group(i)], fac_in.at[i - 1], (group(i), c))) for i in range(1, groups)
    ]
    serve(PLAN[6])
    for item in passed:
        item.wait_recv()
    gram = jnp.zeros((RANK, RANK), F32)
    for j in range(groups):
        block = jnp.concatenate([full[0, j], full[1, j]], axis=0)
        gram = gram + lax.dot_general(block, block, NT, precision=lax.Precision.HIGHEST, preferred_element_type=F32)
    inverse = inverse_factor(gram)
    serve(PLAN[7])
    mine = fac[g]
    for i, item in enumerate(arriving):
        item.wait_recv()
        mine = mine + fac_in[i]
    facs[g] = mine * (1.0 / groups)
    arriving = [begin(copy("xyfacg", i - 1, facs.at[g], facs.at[g], (group(i), c))) for i in range(1, groups)]
    serve(PLAN[8])
    for j in range(groups):
        block = jnp.concatenate([full[0, j], full[1, j]], axis=0)
        l_ref[:, wide * j : wide * (j + 1)] = lax.dot_general(
            inverse, block, NN, precision=lax.Precision.HIGHEST, preferred_element_type=F32
        )
    side_wait(served[0])
    multiply(chips // 2, 3 * chips // 4)
    serve(len(steps))
    side_wait(len(steps))
    multiply(3 * chips // 4, chips)
    for item in arriving:
        item.wait_recv()
    mean = jnp.concatenate(
        [jnp.concatenate([facs[tall * h + j] for j in range(tall)], axis=1) for h in range(2)], axis=0
    )
    r_ref[...] = lax.dot_general(inverse, mean, NN, precision=lax.Precision.HIGHEST, preferred_element_type=F32)
    for item in started:
        item.wait_send()


EARLY = False
PLAN = (3, 4, 6, 7, 9, 10, 11, 12, 13)


def low_rank(groups, chips, rows, grads, prev):
    width, local = rows.shape[1], grads.shape[1]
    wide = width // groups
    counts = dict(
        proj=1, zproj=chips - 1, xysum=groups - 1, zsum=chips - 1, zgat=chips - 1, xygat=groups - 1,
        half=groups, zq=chips - 1, qhalf=chips, xyfac=groups - 1, xyfacg=groups - 1,
    )
    dma = [pltpu.SemaphoreType.DMA((counts[s],)) for s in STAGES]
    chunks = 64 // CHUNK
    ring = pltpu.SemaphoreType.DMA((2, chips // 2, chunks))
    side = pltpu.SemaphoreType.DMA((1 + (chips - 1) * chunks,))
    hbm = pl.BlockSpec(memory_space=pl.ANY)
    vmem = pl.BlockSpec(memory_space=pltpu.VMEM)
    return pl.pallas_call(
        functools.partial(main_kernel, groups, chips),
        out_shape=(
            pltpu.VMEM((RANK, width), F32),
            pltpu.VMEM((RANK, local), F32),
            pltpu.VMEM((width, local), F32),
        ),
        in_specs=[hbm] * 3,
        out_specs=(vmem, vmem, vmem),
        scratch_shapes=[
            pltpu.VMEM((128 * chips, width), BF16),
            pltpu.VMEM((128 * chips, local), BF16),
            pltpu.VMEM((RANK, local), F32),
            pltpu.VMEM((2, chips, HALF, 128), F32),
            pltpu.VMEM((chips, HALF, 128), F32),
            pltpu.VMEM((chips, HALF, 128), F32),
            pltpu.VMEM((chips - 1, HALF, 128), F32),
            pltpu.VMEM((groups, HALF, wide), F32),
            pltpu.VMEM((groups - 1, HALF, wide), F32),
            pltpu.VMEM((chips, 8, 128), F32),
            pltpu.VMEM((chips - 1, 8, 128), F32),
            pltpu.VMEM((chips, 8, 128), F32),
            pltpu.VMEM((2, groups, HALF, wide), F32),
            pltpu.VMEM((2, chips, HALF, 128), F32),
            pltpu.VMEM((groups, HALF, 128), F32),
            pltpu.VMEM((groups - 1, HALF, 128), F32),
            pltpu.VMEM((groups, HALF, 128), F32),
            *dma,
            *dma,
            ring,
            ring,
            side,
            side,
            pltpu.SemaphoreType.DMA((2 + chips,)),
        ],
        compiler_params=pltpu.CompilerParams(collective_id=0, has_side_effects=True, vmem_limit_bytes=40 << 20),
        name="low_rank",
    )(rows, grads, prev)


def residual_kernel(grad_ref, l_ref, r_ref, l_out, r_out, out_ref, left, right, block, sems):
    out = [
        pltpu.make_async_copy(l_ref, l_out, sems.at[0]),
        pltpu.make_async_copy(r_ref, r_out, sems.at[1]),
    ]
    for item in out:
        item.start()
    hi, mid, _ = split3(l_ref[...])
    left[0:RANK] = hi
    left[RANK : 2 * RANK] = hi
    left[2 * RANK :] = mid
    hi, mid, _ = split3(r_ref[...])
    right[0:RANK] = hi
    right[RANK : 2 * RANK] = mid
    right[2 * RANK :] = hi
    slots, size = block.shape[:2]
    for m in range(grad_ref.shape[0] // size):
        at = slice(m * size, (m + 1) * size)
        if m >= slots:
            out[2 + m - slots].wait()
        block[m % slots] = (grad_ref[at] - dot(left[:, at], right[...], TN)).astype(BF16)
        item = pltpu.make_async_copy(block.at[m % slots], out_ref.at[at], sems.at[2 + m % slots])
        item.start()
        out.append(item)
    for item in out[:2] + out[-slots:]:
        item.wait()


def residual(grad, left, right):
    width, local = grad.shape
    size, slots = width // 8, 4
    hbm = pl.BlockSpec(memory_space=pl.ANY)
    vmem = pl.BlockSpec(memory_space=pltpu.VMEM)
    return pl.pallas_call(
        residual_kernel,
        out_shape=(
            jax.ShapeDtypeStruct(left.shape, F32),
            jax.ShapeDtypeStruct(right.shape, F32),
            jax.ShapeDtypeStruct((width, local), BF16),
        ),
        in_specs=[vmem] * 3,
        out_specs=(hbm, hbm, hbm),
        scratch_shapes=[
            pltpu.VMEM((3 * RANK, width), BF16),
            pltpu.VMEM((3 * RANK, local), BF16),
            pltpu.VMEM((slots, size, local), BF16),
            pltpu.SemaphoreType.DMA((2 + slots,)),
        ],
        compiler_params=pltpu.CompilerParams(vmem_limit_bytes=24 << 20),
        name="residual",
    )(grad, left, right)


def body(groups, chips, activations, out_grads, prev_factor):
    left, right, grad = low_rank(groups, chips, activations[0], out_grads[0], prev_factor)
    left, right, rest = residual(grad, left, right)
    return left, right, rest[None]


def solution(mesh):
    placed = (P("dp", "col", None), P("dp", None, "col"), P(None, "col"))
    return jax.shard_map(
        functools.partial(body, mesh.shape["dp"], mesh.shape["col"] // 2),
        mesh=mesh,
        in_specs=placed,
        out_specs=(P(), P(None, "col"), P("dp", None, "col")),
        check_vma=False,
    )
```

time: 502 us -> 86.1 us (0.17)
  waiting for transfers between devices: 408 us -> 0 us
  Pallas kernels: 0 us -> 85.2 us
  matrix products: 60.5 us -> 0 us
  other arithmetic: 13 us -> 0 us
  between operations: 13.8 us -> 0.8 us
  local copies, waits for them, and re-layouts: 5.29 us -> 0 us
    psum x2 -> x0, waiting for transfers between devices: 345 us -> none  [the longest x1 253 us: body(): sketch = lax.psum(partial_sketch, ('dp', 'col')) / groups]
    pallas_call x0 -> x2, Pallas kernels: none -> 85.2 us  [the longest x1 80.9 us: low_rank(): pl.pallas_call(functools.partial(main_kernel, groups, chips), out_shape=(...]
    all_gather x1 -> x0, waiting for transfers between devices: 62 us -> none  [body(): lax.all_gather(local_rows, 'col', axis=0, tiled=True)]
    dot_general x5 -> x0, matrix products: 58.3 us -> none  [the longest x1 15.8 us: body(): lax.dot_general(left_basis, right_factor, (((0,), (0,)), ((), ())), preci...]
    another operation x5 -> x0, other arithmetic: 12.1 us -> none  [the longest x3 6.52 us: body(): factor = jnp.linalg.cholesky(gram)]
    unnamed x10 -> x0, local copies, waits for them, and re-layouts: 5.22 us -> none
  transfers between devices with their start and end apart: 3 -> 0, of which waited for: 3 -> 0; matrix products, arithmetic and copies ran while one was open for 0% -> 0% of each run, Pallas kernels for 0% -> 0%
where the time goes in v2:
time: 86.1 us; the launch traced here: 86 us
  Pallas kernels  85.2 us (99%)
    pallas_call x1, Pallas kernels, low_rank(): pl.pallas_call(functools.partial(main_kernel, groups, chips), out_shape=(...  80.9 us
    pallas_call x1, Pallas kernels, residual(): pl.pallas_call(residual_kernel, out_shape=(jax.ShapeDtypeStruct(left.shap...  4.34 us

profile of v2, /device:TPU:1, one launch (start us, length us, event | category | flops | bytes accessed | tf_op | source)
XLA Modules:
  0.0 86.0 jit_solution(10769725604992985542)
XLA Ops:
  0.6 80.9 %low_rank.1 = (f32[64,4096]{1,0:T(8,128)S(1)}, f32[64,896]{1,0:T(8,128)S(1)}, f32[4096,896]{1,0:T(8,128)S(1)}) custom-call(bf16[64,4096]{1,0:T(8,128)(2,1)} %bitcast.4, bf16[1024,896]{1,0:T(8,128)(2,1)} %bitcast.3, f32[64,896]{1,0:T(8,128)} %p_ref.1), custom_call_target="tpu_custom_call" | custom-call | tf_op jit(solution)/shard_map/low_rank/pallas_call | solution.py:350
  81.5 4.3 %residual.1 = (f32[64,4096]{1,0:T(8,128)}, f32[64,896]{1,0:T(8,128)}, bf16[4096,896]{1,0:T(8,128)(2,1)}) custom-call(f32[4096,896]{1,0:T(8,128)S(1)} %get-tuple-element.9.grad_ref, f32[64,4096]{1,0:T(8,128)S(1)} %get-tuple-element.10.l_ref, f32[64,896]{1,0:T(8,128)S(1)} %get-tuple-element.11.r_ref), custom_call_target="tpu_custom_call" | custom-call | tf_op jit(solution)/shard_map/residual/pallas_call | solution.py:423

commit v3 on v2

--- a/solution.py
+++ b/solution.py
@@ -75,7 +75,7 @@
 
 
 def main_kernel(
-    groups, chips, a_ref, b_ref, p_ref, l_ref, r_ref, grad_ref,
+    groups, chips, a_ref, b_ref, p_ref, l_ref, r_ref, grad_ref, late, late_grads,
     acts, grads, prev, halves, halves_in, psum, psum_in, part, part_in, tile, tile_in, tiles, full, qs, fac, fac_in, facs,
     *sems,
 ):
@@ -115,11 +115,20 @@
         started.append(item)
         return item
 
+    def drain(all_of_them=False):
+        keep = 0 if all_of_them else 3 * groups
+        done = started[: max(0, len(started) - keep)]
+        for item in done:
+            item.wait_send()
+        del started[: len(done)]
+
     chunks = 64 // CHUNK
     last = chips // 2
 
-    def chunk(slot, core, q):
-        return acts.at[pl.ds(pl.multiple_of(128 * slot + 64 * core + CHUNK * q, CHUNK), CHUNK)]
+    def chunk(slot, core, q, rows=CHUNK):
+        early = acts.shape[0] // 128
+        ref, slot = (acts, slot) if slot < early else (late, slot - early)
+        return ref.at[pl.ds(pl.multiple_of(128 * slot + 64 * core + CHUNK * q, CHUNK), rows)]
 
     def ring(way, hop, q):
         offset = hop if way else chips - hop
@@ -139,7 +148,7 @@
     side = []
 
     def pass_on(slot, q, rows=CHUNK):
-        ref = acts.at[pl.ds(pl.multiple_of(128 * slot + 64 * k + CHUNK * q, CHUNK), rows)]
+        ref = chunk(slot, k, q, rows)
         n = len(side)
         side.append(begin(pltpu.make_async_remote_copy(
             src_ref=ref, dst_ref=ref, send_sem=side_send.at[n], recv_sem=side_recv.at[n],
@@ -193,6 +202,7 @@
     own.start()
     for item in loads:
         item.wait()
+    late_grads[...] = grads[96 * chips :]
     proj = fold3(dot(stack3(prev[...]), grads[...], NT), RANK)
     for kk in range(2):
         for s in range(chips):
@@ -202,20 +212,17 @@
 
     send_half = begin(copy("proj", 0, halves.at[1 - k], halves_in, sibling))
     pass_on(0, 0, 64)
-    if EARLY:
-        for q in range(chunks):
-            for way in range(2):
-                ringing[way, 1, q] = begin(ring(way, 1, q))
+    for way in range(2):
+        ringing[way, 1, 0] = begin(ring(way, 1, 0))
     send_half.wait_recv()
 
     psum[...] = halves[k] + halves_in[...]
     arriving = [
         begin(copy("zproj", i - 1, psum.at[slot_of[i]], psum_in.at[i - 1], peer(i))) for i in range(1, chips)
     ]
-    if not EARLY:
-        for q in range(chunks):
-            for way in range(2):
-                ringing[way, 1, q] = begin(ring(way, 1, q))
+    for q in range(1, chunks):
+        for way in range(2):
+            ringing[way, 1, q] = begin(ring(way, 1, q))
     mine = psum[0]
     for i, item in enumerate(arriving):
         item.wait_recv()
@@ -224,11 +231,18 @@
 
     pieces = stack3(mine)
     arriving = []
-    for i in range(1, groups + 1):
-        to = group(i)
-        part[to] = fold3(dot(pieces, acts[:128, pl.ds(pl.multiple_of(wide * to, wide), wide)], NN), HALF)
-        if i < groups:
-            arriving.append(begin(copy("xysum", i - 1, part.at[to], part_in.at[i - 1], (to, c))))
+    for first in range(1, groups + 1, 4):
+        batch = range(first, first + 4)
+        blocks = [
+            fold3(dot(pieces, acts[:128, pl.ds(pl.multiple_of(wide * group(i), wide), wide)], NN), HALF) for i in batch
+        ]
+        for i, block in zip(batch, blocks):
+            part[group(i)] = block
+        for i in batch:
+            if i < groups:
+                arriving.append(
+                    begin(copy("xysum", i - 1, part.at[group(i)], part_in.at[i - 1], (group(i), c)))
+                )
     serve(PLAN[0])
     mine = part[g]
     for i, item in enumerate(arriving):
@@ -254,28 +268,38 @@
     arriving = [begin(copy("xygat", i - 1, full.at[k, g], full.at[k, g], (group(i), c))) for i in range(1, groups)]
     passed = []
 
-    def meet(q, source):
+    def meet(source):
         at = pl.ds(pl.multiple_of(wide * source, wide), wide)
-        return q + dot(stack3(full[k, source]), acts[:128, at], NT)
+        return dot(stack3(full[k, source]), acts[:128, at], NT)
 
     passed.append(begin(copy("half", 0, full.at[k, g], full.at[k, g], sibling)))
-    q = meet(jnp.zeros((3 * HALF, 128), F32), g)
+    q = meet(g)
     serve(PLAN[3])
-    for i, item in enumerate(arriving):
-        item.wait_recv()
-        source = group(groups - (i + 1))
-        passed.append(begin(copy("half", i + 1, full.at[k, source], full.at[k, source], sibling)))
-        q = meet(q, source)
+    for first in range(0, groups - 1, 4):
+        batch = range(first, min(first + 4, groups - 1))
+        if first == groups // 2:
+            serve(PLAN[4])
+        sources = [group(groups - (i + 1)) for i in batch]
+        for i, source in zip(batch, sources):
+            arriving[i].wait_recv()
+            passed.append(begin(copy("half", i + 1, full.at[k, source], full.at[k, source], sibling)))
+        for source in sources:
+            q = q + meet(source)
     qs[k, 0] = fold3(q, HALF)
 
     arriving = [
         begin(copy("zq", i - 1, qs.at[k, 0], qs.at[k, slot_of[chips - i]], peer(i))) for i in range(1, chips)
     ]
     crossing = [begin(copy("qhalf", 0, qs.at[k, 0], qs.at[k, 0], sibling))]
-    serve(PLAN[4])
-    side_wait(served[0])
-    multiply(0, chips // 2)
     serve(PLAN[5])
+    for item in passed:
+        item.wait_recv()
+    gram = jnp.zeros((RANK, RANK), F32)
+    for j in range(groups):
+        block = jnp.concatenate([full[0, j], full[1, j]], axis=0)
+        gram = gram + lax.dot_general(block, block, NT, precision=lax.Precision.HIGHEST, preferred_element_type=F32)
+    inverse = inverse_factor(gram)
+    serve(PLAN[6])
     for i, item in enumerate(arriving):
         item.wait_recv()
         here = qs.at[k, slot_of[chips - (i + 1)]]
@@ -294,22 +318,18 @@
     arriving = [
         begin(copy("xyfac", i - 1, fac.at[group(i)], fac_in.at[i - 1], (group(i), c))) for i in range(1, groups)
     ]
-    serve(PLAN[6])
-    for item in passed:
-        item.wait_recv()
-    gram = jnp.zeros((RANK, RANK), F32)
-    for j in range(groups):
-        block = jnp.concatenate([full[0, j], full[1, j]], axis=0)
-        gram = gram + lax.dot_general(block, block, NT, precision=lax.Precision.HIGHEST, preferred_element_type=F32)
-    inverse = inverse_factor(gram)
     serve(PLAN[7])
+    side_wait(served[0])
+    multiply(0, chips // 2)
+    drain()
+    serve(PLAN[8])
     mine = fac[g]
     for i, item in enumerate(arriving):
         item.wait_recv()
         mine = mine + fac_in[i]
     facs[g] = mine * (1.0 / groups)
     arriving = [begin(copy("xyfacg", i - 1, facs.at[g], facs.at[g], (group(i), c))) for i in range(1, groups)]
-    serve(PLAN[8])
+    serve(PLAN[9])
     for j in range(groups):
         block = jnp.concatenate([full[0, j], full[1, j]], axis=0)
         l_ref[:, wide * j : wide * (j + 1)] = lax.dot_general(
@@ -317,21 +337,19 @@
         )
     side_wait(served[0])
     multiply(chips // 2, 3 * chips // 4)
-    serve(len(steps))
-    side_wait(len(steps))
-    multiply(3 * chips // 4, chips)
+    drain()
     for item in arriving:
         item.wait_recv()
     mean = jnp.concatenate(
         [jnp.concatenate([facs[tall * h + j] for j in range(tall)], axis=1) for h in range(2)], axis=0
     )
     r_ref[...] = lax.dot_general(inverse, mean, NN, precision=lax.Precision.HIGHEST, preferred_element_type=F32)
-    for item in started:
-        item.wait_send()
-
-
-EARLY = False
-PLAN = (3, 4, 6, 7, 9, 10, 11, 12, 13)
+    serve(len(steps))
+    side_wait(len(steps))
+    drain(True)
+
+
+PLAN = (1, 2, 3, 4, 5, 6, 8, 8, 10, 12)
 
 
 def low_rank(groups, chips, rows, grads, prev):
@@ -353,11 +371,13 @@
             pltpu.VMEM((RANK, width), F32),
             pltpu.VMEM((RANK, local), F32),
             pltpu.VMEM((width, local), F32),
+            pltpu.VMEM((32 * chips, width), BF16),
+            pltpu.VMEM((32 * chips, local), BF16),
         ),
         in_specs=[hbm] * 3,
-        out_specs=(vmem, vmem, vmem),
+        out_specs=(vmem,) * 5,
         scratch_shapes=[
-            pltpu.VMEM((128 * chips, width), BF16),
+            pltpu.VMEM((96 * chips, width), BF16),
             pltpu.VMEM((128 * chips, local), BF16),
             pltpu.VMEM((RANK, local), F32),
             pltpu.VMEM((2, chips, HALF, 128), F32),
@@ -382,12 +402,12 @@
             side,
             pltpu.SemaphoreType.DMA((2 + chips,)),
         ],
-        compiler_params=pltpu.CompilerParams(collective_id=0, has_side_effects=True, vmem_limit_bytes=40 << 20),
+        compiler_params=pltpu.CompilerParams(collective_id=0, has_side_effects=True, vmem_limit_bytes=37 << 20),
         name="low_rank",
     )(rows, grads, prev)
 
 
-def residual_kernel(grad_ref, l_ref, r_ref, l_out, r_out, out_ref, left, right, block, sems):
+def residual_kernel(grad_ref, late, late_grads, l_ref, r_ref, l_out, r_out, out_ref, left, right, block, sems):
     out = [
         pltpu.make_async_copy(l_ref, l_out, sems.at[0]),
         pltpu.make_async_copy(r_ref, r_out, sems.at[1]),
@@ -407,7 +427,8 @@
         at = slice(m * size, (m + 1) * size)
         if m >= slots:
             out[2 + m - slots].wait()
-        block[m % slots] = (grad_ref[at] - dot(left[:, at], right[...], TN)).astype(BF16)
+        rest = dot(late[:, at], late_grads[...], TN) - dot(left[:, at], right[...], TN)
+        block[m % slots] = (grad_ref[at] + rest).astype(BF16)
         item = pltpu.make_async_copy(block.at[m % slots], out_ref.at[at], sems.at[2 + m % slots])
         item.start()
         out.append(item)
@@ -415,7 +436,7 @@
         item.wait()
 
 
-def residual(grad, left, right):
+def residual(grad, late, late_grads, left, right):
     width, local = grad.shape
     size, slots = width // 8, 4
     hbm = pl.BlockSpec(memory_space=pl.ANY)
@@ -427,7 +448,7 @@
             jax.ShapeDtypeStruct(right.shape, F32),
             jax.ShapeDtypeStruct((width, local), BF16),
         ),
-        in_specs=[vmem] * 3,
+        in_specs=[vmem] * 5,
         out_specs=(hbm, hbm, hbm),
         scratch_shapes=[
             pltpu.VMEM((3 * RANK, width), BF16),
@@ -435,14 +456,14 @@
             pltpu.VMEM((slots, size, local), BF16),
             pltpu.SemaphoreType.DMA((2 + slots,)),
         ],
-        compiler_params=pltpu.CompilerParams(vmem_limit_bytes=24 << 20),
+        compiler_params=pltpu.CompilerParams(vmem_limit_bytes=16 << 20),
         name="residual",
-    )(grad, left, right)
+    )(grad, late, late_grads, left, right)
 
 
 def body(groups, chips, activations, out_grads, prev_factor):
-    left, right, grad = low_rank(groups, chips, activations[0], out_grads[0], prev_factor)
-    left, right, rest = residual(grad, left, right)
+    left, right, *parts = low_rank(groups, chips, activations[0], out_grads[0], prev_factor)
+    left, right, rest = residual(*parts, left, right)
     return left, right, rest[None]
 
 

time: 86.1 us -> 79.3 us (0.921)
  Pallas kernels: 85.2 us -> 78.4 us
    pallas_call x1, Pallas kernels: 80.9 us -> 71.9 us  [low_rank(): pl.pallas_call(functools.partial(main_kernel, groups, chips), out_shape=(...]
    pallas_call x1, Pallas kernels: 4.34 us -> 6.49 us  [residual(): pl.pallas_call(residual_kernel, out_shape=(jax.ShapeDtypeStruct(left.shap...]
where the time goes in v3:
time: 79.3 us; the launch traced here: 79.2 us
  Pallas kernels  78.4 us (99%)
  between operations  0.8 us (1%)
    pallas_call x1, Pallas kernels, low_rank(): pl.pallas_call(functools.partial(main_kernel, groups, chips), out_shape=(...  71.9 us
    pallas_call x1, Pallas kernels, residual(): pl.pallas_call(residual_kernel, out_shape=(jax.ShapeDtypeStruct(left.shap...  6.49 us

profile of v3, /device:TPU:1, one launch (start us, length us, event | category | flops | bytes accessed | tf_op | source)
XLA Modules:
  0.0 79.2 jit_solution(11818089284388612395)
XLA Ops:
  0.6 71.9 %low_rank.1 = (f32[64,4096]{1,0:T(8,128)S(1)}, f32[64,896]{1,0:T(8,128)S(1)}, f32[4096,896]{1,0:T(8,128)S(1)}, bf16[256,4096]{1,0:T(8,128)(2,1)S(1)}, bf16[256,896]{1,0:T(8,128)(2,1)S(1)}) custom-call(bf16[64,4096]{1,0:T(8,128)(2,1)} %bitcast.4, bf16[1024,896]{1,0:T(8,128)(2,1)} %bitcast.3, f32[64,896]{1,0:T(8,128)} %p_ref.1), custom_call_target="tpu_custom_call" | custom-call | tf_op jit(solution)/shard_map/low_rank/pallas_call | solution.py:368
  72.6 6.5 %residual.1 = (f32[64,4096]{1,0:T(8,128)}, f32[64,896]{1,0:T(8,128)}, bf16[4096,896]{1,0:T(8,128)(2,1)}) custom-call(f32[4096,896]{1,0:T(8,128)S(1)} %get-tuple-element.11.grad_ref, bf16[256,4096]{1,0:T(8,128)(2,1)S(1)} %get-tuple-element.12.late, bf16[256,896]{1,0:T(8,128)(2,1)S(1)} %get-tuple-element.13.late_grads, ...), custom_call_target="tpu_custom_call" | custom-call | tf_op jit(solution)/shard_map/residual/pallas_call | solution.py:444

commit v4 on v3

--- a/solution.py
+++ b/solution.py
@@ -1,4 +1,5 @@
 import functools
+import math
 
 import jax
 import jax.numpy as jnp
@@ -75,7 +76,7 @@
 
 
 def main_kernel(
-    groups, chips, a_ref, b_ref, p_ref, l_ref, r_ref, grad_ref, late, late_grads,
+    groups, chips, a_ref, b_ref, p_ref, l_ref, r_ref, left, right, grad_ref, late, late_grads,
     acts, grads, prev, halves, halves_in, psum, psum_in, part, part_in, tile, tile_in, tiles, full, qs, fac, fac_in, facs,
     *sems,
 ):
@@ -99,8 +100,15 @@
     def peer(offset):
         return (g, 2 * chip(offset) + k)
 
-    def group(offset):
-        return lax.rem(g + offset, groups)
+    edge = math.isqrt(groups)
+    moves = [(dx, dy) for dx in range(edge) for dy in range(edge)]
+    moves.sort(key=lambda move: -sum(min(d, edge - d) for d in move))
+    far_first = sorted(range(1, chips), key=lambda i: -min(i, chips - i))
+
+    def group(i, sign=1):
+        dx, dy = moves[i - 1]
+        x, y = lax.rem(g // edge + sign * dx + edge, edge), lax.rem(lax.rem(g, edge) + sign * dy + edge, edge)
+        return x * edge + y
 
     def copy(stage, slot, src, dst, device):
         return pltpu.make_async_remote_copy(
@@ -116,7 +124,7 @@
         return item
 
     def drain(all_of_them=False):
-        keep = 0 if all_of_them else 3 * groups
+        keep = 0 if all_of_them else 2 * groups
         done = started[: max(0, len(started) - keep)]
         for item in done:
             item.wait_send()
@@ -218,15 +226,15 @@
 
     psum[...] = halves[k] + halves_in[...]
     arriving = [
-        begin(copy("zproj", i - 1, psum.at[slot_of[i]], psum_in.at[i - 1], peer(i))) for i in range(1, chips)
+        begin(copy("zproj", i - 1, psum.at[slot_of[i]], psum_in.at[i - 1], peer(i))) for i in far_first
     ]
     for q in range(1, chunks):
         for way in range(2):
             ringing[way, 1, q] = begin(ring(way, 1, q))
     mine = psum[0]
-    for i, item in enumerate(arriving):
-        item.wait_recv()
-        mine = mine + psum_in[i]
+    for i, item in zip(far_first[::-1], arriving[::-1]):
+        item.wait_recv()
+        mine = mine + psum_in[i - 1]
     side_wait(0)
 
     pieces = stack3(mine)
@@ -251,14 +259,14 @@
 
     for j in range(chips):
         tile[j] = mine[8 * (j // cols) : 8 * (j // cols + 1), 128 * (j % cols) : 128 * (j % cols + 1)]
-    arriving = [begin(copy("zsum", i - 1, tile.at[chip(i)], tile_in.at[i - 1], peer(i))) for i in range(1, chips)]
+    arriving = [begin(copy("zsum", i - 1, tile.at[chip(i)], tile_in.at[i - 1], peer(i))) for i in far_first]
     serve(PLAN[1])
     mine = tile[z]
-    for i, item in enumerate(arriving):
-        item.wait_recv()
-        mine = mine + tile_in[i]
+    for i, item in zip(far_first[::-1], arriving[::-1]):
+        item.wait_recv()
+        mine = mine + tile_in[i - 1]
     tiles[z] = mine * (1.0 / groups)
-    arriving = [begin(copy("zgat", i - 1, tiles.at[z], tiles.at[z], peer(i))) for i in range(1, chips)]
+    arriving = [begin(copy("zgat", i - 1, tiles.at[z], tiles.at[z], peer(i))) for i in far_first]
     serve(PLAN[2])
     for item in arriving:
         item.wait_recv()
@@ -275,11 +283,12 @@
     passed.append(begin(copy("half", 0, full.at[k, g], full.at[k, g], sibling)))
     q = meet(g)
     serve(PLAN[3])
+    near_first = list(range(groups - 1))[::-1]
     for first in range(0, groups - 1, 4):
-        batch = range(first, min(first + 4, groups - 1))
+        batch = near_first[first : first + 4]
         if first == groups // 2:
             serve(PLAN[4])
-        sources = [group(groups - (i + 1)) for i in batch]
+        sources = [group(i + 1, -1) for i in batch]
         for i, source in zip(batch, sources):
             arriving[i].wait_recv()
             passed.append(begin(copy("half", i + 1, full.at[k, source], full.at[k, source], sibling)))
@@ -288,7 +297,7 @@
     qs[k, 0] = fold3(q, HALF)
 
     arriving = [
-        begin(copy("zq", i - 1, qs.at[k, 0], qs.at[k, slot_of[chips - i]], peer(i))) for i in range(1, chips)
+        begin(copy("zq", i - 1, qs.at[k, 0], qs.at[k, slot_of[chips - i]], peer(i))) for i in far_first
     ]
     crossing = [begin(copy("qhalf", 0, qs.at[k, 0], qs.at[k, 0], sibling))]
     serve(PLAN[5])
@@ -300,10 +309,10 @@
         gram = gram + lax.dot_general(block, block, NT, precision=lax.Precision.HIGHEST, preferred_element_type=F32)
     inverse = inverse_factor(gram)
     serve(PLAN[6])
-    for i, item in enumerate(arriving):
-        item.wait_recv()
-        here = qs.at[k, slot_of[chips - (i + 1)]]
-        crossing.append(begin(copy("qhalf", i + 1, here, here, sibling)))
+    for i, item in zip(far_first[::-1], arriving[::-1]):
+        item.wait_recv()
+        here = qs.at[k, slot_of[chips - i]]
+        crossing.append(begin(copy("qhalf", i, here, here, sibling)))
     for item in crossing:
         item.wait_recv()
     q = jnp.concatenate([jnp.concatenate([qs[0, s], qs[1, s]], axis=0) for s in range(chips)], axis=1)
@@ -332,9 +341,11 @@
     serve(PLAN[9])
     for j in range(groups):
         block = jnp.concatenate([full[0, j], full[1, j]], axis=0)
-        l_ref[:, wide * j : wide * (j + 1)] = lax.dot_general(
-            inverse, block, NN, precision=lax.Precision.HIGHEST, preferred_element_type=F32
-        )
+        at = slice(wide * j, wide * (j + 1))
+        block = lax.dot_general(inverse, block, NN, precision=lax.Precision.HIGHEST, preferred_element_type=F32)
+        l_ref[:, at] = block
+        hi, mid, _ = split3(block)
+        left[:, at] = jnp.concatenate([hi, hi, mid], axis=0)
     side_wait(served[0])
     multiply(chips // 2, 3 * chips // 4)
     drain()
@@ -343,13 +354,16 @@
     mean = jnp.concatenate(
         [jnp.concatenate([facs[tall * h + j] for j in range(tall)], axis=1) for h in range(2)], axis=0
     )
-    r_ref[...] = lax.dot_general(inverse, mean, NN, precision=lax.Precision.HIGHEST, preferred_element_type=F32)
+    mean = lax.dot_general(inverse, mean, NN, precision=lax.Precision.HIGHEST, preferred_element_type=F32)
+    r_ref[...] = mean
+    hi, mid, _ = split3(mean)
+    right[...] = jnp.concatenate([hi, mid, hi], axis=0)
     serve(len(steps))
     side_wait(len(steps))
     drain(True)
 
 
-PLAN = (1, 2, 3, 4, 5, 6, 8, 8, 10, 12)
+PLAN = (1, 1, 2, 4, 5, 6, 8, 8, 10, 12)
 
 
 def low_rank(groups, chips, rows, grads, prev):
@@ -370,12 +384,14 @@
         out_shape=(
             pltpu.VMEM((RANK, width), F32),
             pltpu.VMEM((RANK, local), F32),
+            pltpu.VMEM((3 * RANK, width), BF16),
+            pltpu.VMEM((3 * RANK, local), BF16),
             pltpu.VMEM((width, local), F32),
             pltpu.VMEM((32 * chips, width), BF16),
             pltpu.VMEM((32 * chips, local), BF16),
         ),
         in_specs=[hbm] * 3,
-        out_specs=(vmem,) * 5,
+        out_specs=(vmem,) * 7,
         scratch_shapes=[
             pltpu.VMEM((96 * chips, width), BF16),
             pltpu.VMEM((128 * chips, local), BF16),
@@ -407,21 +423,13 @@
     )(rows, grads, prev)
 
 
-def residual_kernel(grad_ref, late, late_grads, l_ref, r_ref, l_out, r_out, out_ref, left, right, block, sems):
+def residual_kernel(l_ref, r_ref, left, right, grad_ref, late, late_grads, l_out, r_out, out_ref, block, sems):
     out = [
         pltpu.make_async_copy(l_ref, l_out, sems.at[0]),
         pltpu.make_async_copy(r_ref, r_out, sems.at[1]),
     ]
     for item in out:
         item.start()
-    hi, mid, _ = split3(l_ref[...])
-    left[0:RANK] = hi
-    left[RANK : 2 * RANK] = hi
-    left[2 * RANK :] = mid
-    hi, mid, _ = split3(r_ref[...])
-    right[0:RANK] = hi
-    right[RANK : 2 * RANK] = mid
-    right[2 * RANK :] = hi
     slots, size = block.shape[:2]
     for m in range(grad_ref.shape[0] // size):
         at = slice(m * size, (m + 1) * size)
@@ -436,7 +444,8 @@
         item.wait()
 
 
-def residual(grad, late, late_grads, left, right):
+def residual(*parts):
+    left, right, _, _, grad, _, _ = parts
     width, local = grad.shape
     size, slots = width // 8, 4
     hbm = pl.BlockSpec(memory_space=pl.ANY)
@@ -448,22 +457,20 @@
             jax.ShapeDtypeStruct(right.shape, F32),
             jax.ShapeDtypeStruct((width, local), BF16),
         ),
-        in_specs=[vmem] * 5,
+        in_specs=[vmem] * 7,
         out_specs=(hbm, hbm, hbm),
         scratch_shapes=[
-            pltpu.VMEM((3 * RANK, width), BF16),
-            pltpu.VMEM((3 * RANK, local), BF16),
             pltpu.VMEM((slots, size, local), BF16),
             pltpu.SemaphoreType.DMA((2 + slots,)),
         ],
         compiler_params=pltpu.CompilerParams(vmem_limit_bytes=16 << 20),
         name="residual",
-    )(grad, late, late_grads, left, right)
+    )(*parts)
 
 
 def body(groups, chips, activations, out_grads, prev_factor):
-    left, right, *parts = low_rank(groups, chips, activations[0], out_grads[0], prev_factor)
-    left, right, rest = residual(*parts, left, right)
+    parts = low_rank(groups, chips, activations[0], out_grads[0], prev_factor)
+    left, right, rest = residual(*parts)
     return left, right, rest[None]
 
 

time: 79.3 us -> 77.8 us (0.981)
  Pallas kernels: 78.4 us -> 76.9 us
    pallas_call x1, Pallas kernels: 71.9 us -> 70.5 us  [low_rank(): pl.pallas_call(functools.partial(main_kernel, groups, chips), out_shape=(...]
where the time goes in v4:
time: 77.8 us; the launch traced here: 77.7 us
  Pallas kernels  76.9 us (99%)
  between operations  0.8 us (1%)
    pallas_call x1, Pallas kernels, low_rank(): pl.pallas_call(functools.partial(main_kernel, groups, chips), out_shape=(...  70.5 us
    pallas_call x1, Pallas kernels, residual(): pl.pallas_call(residual_kernel, out_shape=(jax.ShapeDtypeStruct(left.shap...  6.39 us

profile of v4, /device:TPU:1, one launch (start us, length us, event | category | flops | bytes accessed | tf_op | source)
XLA Modules:
  0.0 77.7 jit_solution(1297681533967721840)
XLA Ops:
  0.6 70.5 %low_rank.1 = (f32[64,4096]{1,0:T(8,128)S(1)}, f32[64,896]{1,0:T(8,128)S(1)}, bf16[192,4096]{1,0:T(8,128)(2,1)S(1)}, bf16[192,896]{1,0:T(8,128)(2,1)S(1)}, f32[4...) custom-call(bf16[64,4096]{1,0:T(8,128)(2,1)} %bitcast.4, ...), custom_call_target="tpu_custom_call" | custom-call | tf_op jit(solution)/shard_map/low_rank/pallas_call | solution.py:382
  71.2 6.4 %residual.1 = (f32[64,4096]{1,0:T(8,128)}, f32[64,896]{1,0:T(8,128)}, bf16[4096,896]{1,0:T(8,128)(2,1)}) custom-call(f32[64,4096]{1,0:T(8,128)S(1)} %get-tuple-element.13.l_ref, f32[64,896]{1,0:T(8,128)S(1)} %get-tuple-element.14.r_ref, bf16[192,4096]{1,0:T(8,128)(2,1)S(1)} %get-tuple-element.15.left, bf16[192,896]{1,0:T(8,128)(2,1)S(1)} %get-tuple-element.16.right, ...), custom_call_target="tpu_custom_call" | custom-call | tf_op jit(solution)/shard_map/residual/pallas_call | solution.py:453

commit v5 on v4

--- a/solution.py
+++ b/solution.py
@@ -149,8 +149,8 @@
 
     steps = []
     for hop in range(1, last):
-        steps += [[(0, hop, q), (1, hop, q)] for q in range(chunks)]
-    steps += [[(0, last, q), (1, last, q + chunks // 2)] for q in range(chunks // 2)]
+        steps += [[(0, hop, q), (1, hop, chunks - 1 - q)] for q in range(chunks)]
+    steps += [[(0, last, q), (1, last, chunks - 1 - q)] for q in range(chunks // 2)]
     final = {item for step in steps for item in step if item[1] == last}
     served = [0]
     side = []
@@ -220,17 +220,16 @@
 
     send_half = begin(copy("proj", 0, halves.at[1 - k], halves_in, sibling))
     pass_on(0, 0, 64)
-    for way in range(2):
-        ringing[way, 1, 0] = begin(ring(way, 1, 0))
+    for item in steps[0]:
+        ringing[item] = begin(ring(*item))
     send_half.wait_recv()
 
     psum[...] = halves[k] + halves_in[...]
     arriving = [
         begin(copy("zproj", i - 1, psum.at[slot_of[i]], psum_in.at[i - 1], peer(i))) for i in far_first
     ]
-    for q in range(1, chunks):
-        for way in range(2):
-            ringing[way, 1, q] = begin(ring(way, 1, q))
+    for item in sum(steps[1:chunks], []):
+        ringing[item] = begin(ring(*item))
     mine = psum[0]
     for i, item in zip(far_first[::-1], arriving[::-1]):
         item.wait_recv()
@@ -329,7 +328,9 @@
     ]
     serve(PLAN[7])
     side_wait(served[0])
-    multiply(0, chips // 2)
+    multiply(0, chips // 4)
+    serve(9)
+    multiply(chips // 4, chips // 2)
     drain()
     serve(PLAN[8])
     mine = fac[g]
@@ -363,7 +364,7 @@
     drain(True)
 
 
-PLAN = (1, 1, 2, 4, 5, 6, 8, 8, 10, 12)
+PLAN = (1, 1, 3, 4, 5, 6, 8, 8, 10, 12)
 
 
 def low_rank(groups, chips, rows, grads, prev):

time: 77.8 us -> 76.8 us (0.987)
  Pallas kernels: 76.9 us -> 75.9 us
    pallas_call x1, Pallas kernels: 70.5 us -> 69.5 us  [low_rank(): pl.pallas_call(functools.partial(main_kernel, groups, chips), out_shape=(...]
where the time goes in v5:
time: 76.8 us; the launch traced here: 76.7 us
  Pallas kernels  75.9 us (99%)
  between operations  0.8 us (1%)
    pallas_call x1, Pallas kernels, low_rank(): pl.pallas_call(functools.partial(main_kernel, groups, chips), out_shape=(...  69.5 us
    pallas_call x1, Pallas kernels, residual(): pl.pallas_call(residual_kernel, out_shape=(jax.ShapeDtypeStruct(left.shap...  6.39 us

profile of v5, /device:TPU:1, one launch (start us, length us, event | category | flops | bytes accessed | tf_op | source)
XLA Modules:
  0.0 76.7 jit_solution(2814781892574822740)
XLA Ops:
  0.6 69.5 %low_rank.1 = (f32[64,4096]{1,0:T(8,128)S(1)}, f32[64,896]{1,0:T(8,128)S(1)}, bf16[192,4096]{1,0:T(8,128)(2,1)S(1)}, bf16[192,896]{1,0:T(8,128)(2,1)S(1)}, f32[4...) custom-call(bf16[64,4096]{1,0:T(8,128)(2,1)} %bitcast.4, ...), custom_call_target="tpu_custom_call" | custom-call | tf_op jit(solution)/shard_map/low_rank/pallas_call | solution.py:383
  70.2 6.4 %residual.1 = (f32[64,4096]{1,0:T(8,128)}, f32[64,896]{1,0:T(8,128)}, bf16[4096,896]{1,0:T(8,128)(2,1)}) custom-call(f32[64,4096]{1,0:T(8,128)S(1)} %get-tuple-element.13.l_ref, f32[64,896]{1,0:T(8,128)S(1)} %get-tuple-element.14.r_ref, bf16[192,4096]{1,0:T(8,128)(2,1)S(1)} %get-tuple-element.15.left, bf16[192,896]{1,0:T(8,128)(2,1)S(1)} %get-tuple-element.16.right, ...), custom_call_target="tpu_custom_call" | custom-call | tf_op jit(solution)/shard_map/residual/pallas_call | solution.py:454
